TPU v7x, 32 devices: a whole 2x2x4 slice. The times are simulated.
32 devices in a mesh: dp: 16 (over z, x, core), mp: 2 (over y).
Axes of the slice: x: 2, y: 2, z: 4, core: 2. Of those that a mesh axis runs over, the one named last changes fastest.
Arguments:
- kernel_state: float32 [3, 1024, 2304], P(None, 'mp'), may hold values from -2 to 2, as said below
- qkv_state: float32 [3, 768, 2304], P(None, 'dp', 'mp'), may hold values from -2 to 2, as said below
- proj_state: float32 [3, 768, 768], P(None, 'dp', 'mp'), may hold values from -4 to 4, as said below
- fc1_state: float32 [3, 768, 3072], P(None, 'dp', 'mp'), may hold values from -2 to 2, as said below
- fc2_state: float32 [3, 3072, 768], P(None, 'dp', 'mp'), may hold values from -2 to 2, as said below
- table_state: float32 [3, 60, 768], replicated, may hold values from -4 to 8, as said below
- patches_s: bfloat16 [32, 784, 192], P('dp'), may hold values from -6 to 6
- patches_l: bfloat16 [64, 16, 6912], P('dp'), may hold values from -6 to 6
- resize_s: float32 [64, 1024], P(None, 'mp'), may hold values from -2 to 2
- resize_l: float32 [2304, 1024], P(None, 'mp'), may hold values from -0.3125 to 0.3125
- bilin_s: float32 [784, 49], replicated, may hold values from 0 to 0.040816326
- bilin_l: float32 [16, 49], replicated, may hold values from 0 to 0.040816326
- cotangent: float32 [26112, 768], P(('dp', 'mp')), may hold values from -6 to 6
- rates: float32 [6], replicated, may hold values from 0 to 2, as said below
- step: int32 [1], replicated, may hold values from 1 to 3
Outputs:
- block_out: float32 [26112, 768], P(('dp', 'mp'))
- grad_norm: float32 [], replicated
- kernel_new: float32 [1024, 2304], P('mp')
- kernel_moments: float32 [2, 1024, 2304], P(None, 'mp')
- qkv_new: float32 [768, 2304], P('dp', 'mp')
- qkv_moments: float32 [2, 768, 2304], P(None, 'dp', 'mp')
- proj_new: float32 [768, 768], P('dp', 'mp')
- proj_moments: float32 [2, 768, 768], P(None, 'dp', 'mp')
- fc1_new: float32 [768, 3072], P('dp', 'mp')
- fc1_moments: float32 [2, 768, 3072], P(None, 'dp', 'mp')
- fc2_new: float32 [3072, 768], P('dp', 'mp')
- fc2_moments: float32 [2, 3072, 768], P(None, 'dp', 'mp')
- table_new: float32 [60, 768], replicated
- table_moments: float32 [2, 60, 768], replicated
Inputs may be any that keep to these rules, and one draw needn't show every extreme that they name: `kernel_state`: entry 2 of every state (the second moment) is positive. `qkv_state`: entry 2 is positive. `proj_state`: entry 2 is positive. `fc1_state`: entry 2 is positive. `fc2_state`: entry 2 is positive. `table_state`: entry 2 is positive. `rates`: Positive.
All inputs are finite; a program needn't handle non-finite values.
Results may differ from a plain program's by a relative error of at most 0.019.
Values may be sent and summed in bfloat16 or wider, within the bound.
No kernel may reach another device: no remote copies, remote signals or barrier semaphores. Data moves between devices by JAX's collectives and lax.ppermute only.
A program may use at most 256 MiB of HBM per device.

v0:
```python
import math
import jax
import jax.numpy as jnp
from jax import lax
from jax.sharding import PartitionSpec as P

D = 768
HEADS = 12
HEAD_DIM = 64
FF = 3072
BASE = 32
POS_GRID = 7
GRID_S = 28
GRID_L = 4
TROWS = 60
HIGHEST = lax.Precision.HIGHEST
NORM_EPS = 1e-06
BETA_ONE = 0.5
BETA_TWO = 0.5
DECAY = 0.05
ADAM_EPS = 1e-08
MASKED = -1e30


def to_low(array_in):
    return array_in.astype(jnp.bfloat16)


def matmul(left, right):
    return jnp.dot(left, right, preferred_element_type=jnp.float32)


def matmul_left(left, right):
    return lax.dot_general(
        left, right, (((0,), (0,)), ((), ())), preferred_element_type=jnp.float32
    )


def matmul_right(left, right):
    return lax.dot_general(
        left, right, (((1,), (1,)), ((), ())), preferred_element_type=jnp.float32
    )


def exact_left(left, right):
    return lax.dot_general(
        left, right, (((0,), (0,)), ((), ())), precision=HIGHEST, preferred_element_type=jnp.float32
    )


def norm_forward(inputs):
    centered = inputs - jnp.mean(inputs, axis=-1, keepdims=True)
    inverse = lax.rsqrt(jnp.mean(centered * centered, axis=-1, keepdims=True) + NORM_EPS)
    return (centered * inverse, inverse)


def norm_backward(upstream, normalized, inverse, gain_row):
    scaled = upstream * gain_row
    inner = jnp.mean(scaled * normalized, axis=-1, keepdims=True)
    result = inverse * (scaled - jnp.mean(scaled, axis=-1, keepdims=True) - normalized * inner)
    return (result, jnp.sum(upstream * normalized, axis=0), jnp.sum(upstream, axis=0))


def gelu_exact(inputs):
    return 0.5 * inputs * (1.0 + lax.erf(inputs * 0.7071067811865476))


def gelu_slope(inputs):
    return (
        0.5 * (1.0 + lax.erf(inputs * 0.7071067811865476))
        + inputs * jnp.exp(-0.5 * inputs * inputs) * 0.3989422804014327
    )


def image_ids(row_count):
    places = jnp.arange(row_count, dtype=jnp.int32)
    first_row = GRID_S * GRID_S
    return jnp.where(places < first_row, 0, 1 + (places - first_row) // (GRID_L * GRID_L))


def adam_step(state_stack, gradient, rate_value, factor, fix_one, fix_two):
    clipped = gradient * factor
    first_moment = BETA_ONE * state_stack[1] + (1.0 - BETA_ONE) * clipped
    second = BETA_TWO * state_stack[2] + (1.0 - BETA_TWO) * clipped * clipped
    movement = (
        first_moment / fix_one / (jnp.sqrt(second / fix_two) + ADAM_EPS) + DECAY * state_stack[0]
    )
    return (state_stack[0] - rate_value * movement, jnp.stack([first_moment, second]))


def body(
    kernel_state,
    qkv_state,
    proj_state,
    fc1_state,
    fc2_state,
    table_state,
    patches_s,
    patches_l,
    resize_s,
    resize_l,
    bilin_s,
    bilin_l,
    cotangent,
    rates,
    step,
):
    group_size = lax.axis_size("mp")
    qkv_low = to_low(qkv_state[0])
    proj_low = to_low(proj_state[0])
    fc1_low = to_low(fc1_state[0])
    fc2_low = to_low(fc2_state[0])
    by_rows = (
        lax.all_gather(qkv_low, "dp", axis=0, tiled=True),
        lax.all_gather(proj_low, "dp", axis=0, tiled=True),
        lax.all_gather(fc1_low, "dp", axis=0, tiled=True),
        lax.all_gather(fc2_low, "dp", axis=0, tiled=True),
    )
    w_qkv, w_proj, w_fc1, w_fc2 = (
        lax.all_gather(by_rows[0], "mp", axis=1, tiled=True),
        lax.all_gather(by_rows[1], "mp", axis=1, tiled=True),
        lax.all_gather(by_rows[2], "mp", axis=1, tiled=True),
        lax.all_gather(by_rows[3], "mp", axis=1, tiled=True),
    )
    base_rows = kernel_state[0]
    width = base_rows.shape[1] // 3
    small_flat = patches_s.reshape(-1, patches_s.shape[2])
    large_flat = patches_l.reshape(-1, patches_l.shape[2])
    small_tokens = patches_s.shape[1]
    large_tokens = patches_l.shape[0] * patches_l.shape[1] // group_size
    part_small = jnp.dot(resize_s, base_rows, precision=HIGHEST).reshape(-1, width)
    part_large = jnp.dot(resize_l, base_rows, precision=HIGHEST).reshape(-1, width)
    kern_small, kern_large = (
        lax.psum_scatter(part_small, "mp", scatter_dimension=1, tiled=True),
        lax.psum_scatter(part_large, "mp", scatter_dimension=1, tiled=True),
    )
    embed_small = matmul(small_flat, to_low(kern_small)).reshape(group_size, small_tokens, -1)
    embed_large = jnp.dot(large_flat.astype(jnp.float32), kern_large, precision=HIGHEST).reshape(
        group_size, large_tokens, -1
    )
    relaid = lax.all_to_all(
        jnp.concatenate([embed_small, embed_large], axis=1),
        "mp",
        split_axis=0,
        concat_axis=2,
        tiled=True,
    )
    embedded = relaid[0]
    table_rows = table_state[0]
    first_row = POS_GRID * POS_GRID
    grid_rows = table_rows[:first_row]
    pos_small = jnp.dot(bilin_s, grid_rows, precision=HIGHEST)
    pos_large = jnp.dot(bilin_l, grid_rows, precision=HIGHEST)
    images_large = large_tokens // bilin_l.shape[0]
    placed = (
        jnp.concatenate([pos_small, jnp.tile(pos_large, (images_large, 1))], axis=0)
        + table_rows[first_row]
    )
    inputs = embedded + placed
    row_count = inputs.shape[0]
    normal_one, inverse_one = norm_forward(inputs)
    normed_one = to_low(normal_one * table_rows[first_row + 1] + table_rows[first_row + 2])
    qkv_rows = to_low(matmul(normed_one, w_qkv))
    split_heads = qkv_rows.reshape(row_count, 3, HEADS, HEAD_DIM).transpose(1, 2, 0, 3)
    labels = image_ids(row_count)
    same_image = labels[:, None] == labels[None, :]
    scale = HEAD_DIM ** (-0.5)

    def head_scores(queries, key_rows):
        raw_scores = matmul_right(queries, key_rows) * scale
        return jnp.where(same_image, raw_scores, MASKED)

    def attend_head(pieces):
        scores = head_scores(pieces[0], pieces[1])
        largest = jnp.max(scores, axis=1, keepdims=True)
        exponent = jnp.exp(scores - largest)
        totals = jnp.sum(exponent, axis=1, keepdims=True)
        attended_head = matmul(to_low(exponent / totals), pieces[2])
        return (attended_head, (largest + jnp.log(totals))[:, 0])

    head_out, log_totals = lax.map(attend_head, (split_heads[0], split_heads[1], split_heads[2]))
    attended = to_low(head_out.transpose(1, 0, 2).reshape(row_count, -1))
    middle = inputs + matmul(attended, w_proj) + table_rows[first_row + 5]
    normal_two, inverse_two = norm_forward(middle)
    normed_two = to_low(normal_two * table_rows[first_row + 3] + table_rows[first_row + 4])
    hidden = matmul(normed_two, w_fc1) + table_rows[first_row + 7 :].reshape(-1)
    activated = to_low(gelu_exact(hidden))
    block_out = middle + matmul(activated, w_fc2) + table_rows[first_row + 6]
    upstream_low = to_low(cotangent)
    grad_fc2 = matmul_left(activated, upstream_low)
    bias_two_grad = jnp.sum(upstream_low.astype(jnp.float32), axis=0)
    hidden_grad = to_low(matmul_right(upstream_low, w_fc2) * gelu_slope(hidden))
    grad_fc1 = matmul_left(normed_two, hidden_grad)
    bias_one_grad = jnp.sum(hidden_grad.astype(jnp.float32), axis=0)
    norm_two_grad, gain_two_grad, shift_two_grad = norm_backward(
        matmul_right(hidden_grad, w_fc1), normal_two, inverse_two, table_rows[first_row + 3]
    )
    middle_grad = cotangent + norm_two_grad
    branch_low = to_low(middle_grad)
    grad_proj = matmul_left(attended, branch_low)
    bias_proj_grad = jnp.sum(branch_low.astype(jnp.float32), axis=0)
    attended_grad = (
        to_low(matmul_right(branch_low, w_proj))
        .reshape(row_count, HEADS, HEAD_DIM)
        .transpose(1, 0, 2)
    )

    def attend_back(pieces):
        queries, key_rows, value_rows, totals_log, out_grad = pieces
        probs = jnp.exp(head_scores(queries, key_rows) - totals_log[:, None])
        prob_grad = matmul_right(out_grad, value_rows)
        value_grad = matmul_left(to_low(probs), out_grad)
        score_grad = to_low(probs * (prob_grad - jnp.sum(probs * prob_grad, axis=1, keepdims=True)))
        return jnp.stack(
            [
                matmul(score_grad, key_rows) * scale,
                matmul_left(score_grad, queries) * scale,
                value_grad,
            ]
        )

    head_grads = lax.map(
        attend_back, (split_heads[0], split_heads[1], split_heads[2], log_totals, attended_grad)
    )
    qkv_grad = to_low(head_grads.transpose(2, 1, 0, 3).reshape(row_count, -1))
    grad_qkv = matmul_left(normed_one, qkv_grad)
    norm_one_grad, gain_one_grad, shift_one_grad = norm_backward(
        matmul_right(qkv_grad, w_qkv), normal_one, inverse_one, table_rows[first_row + 1]
    )
    input_grad = middle_grad + norm_one_grad
    large_grad = (
        input_grad[small_tokens:].reshape(images_large, -1, input_grad.shape[1]).sum(axis=0)
    )
    pos_grad = exact_left(bilin_s, input_grad[:small_tokens]) + exact_left(bilin_l, large_grad)
    vector_grads = jnp.stack(
        [
            jnp.sum(input_grad, axis=0),
            gain_one_grad,
            shift_one_grad,
            gain_two_grad,
            shift_two_grad,
            bias_proj_grad,
            bias_two_grad,
        ]
    )
    table_grad = jnp.concatenate(
        [pos_grad, vector_grads, bias_one_grad.reshape(-1, input_grad.shape[1])], axis=0
    )
    grad_low = to_low(input_grad)
    returned = lax.all_to_all(grad_low[None], "mp", split_axis=2, concat_axis=0, tiled=True)
    kern_small_grad = matmul_left(
        small_flat, returned[:, :small_tokens].reshape(-1, returned.shape[2])
    )
    kern_large_grad = matmul_left(
        large_flat, returned[:, small_tokens:].reshape(-1, returned.shape[2])
    )
    summed_small, summed_large = (
        lax.psum(kern_small_grad.astype(jnp.bfloat16), "dp").astype(jnp.float32),
        lax.psum(kern_large_grad.astype(jnp.bfloat16), "dp").astype(jnp.float32),
    )
    whole_small, whole_large = (
        lax.all_gather(summed_small.astype(jnp.bfloat16), "mp", axis=1, tiled=True).astype(
            summed_small.dtype
        ),
        lax.all_gather(summed_large.astype(jnp.bfloat16), "mp", axis=1, tiled=True).astype(
            summed_large.dtype
        ),
    )
    base_grad = exact_left(resize_s, whole_small.reshape(resize_s.shape[0], -1)) + exact_left(
        resize_l, whole_large.reshape(resize_l.shape[0], -1)
    )
    rows_summed = (
        lax.psum_scatter(
            grad_qkv.astype(jnp.bfloat16), "dp", scatter_dimension=0, tiled=True
        ).astype(jnp.float32),
        lax.psum_scatter(
            grad_proj.astype(jnp.bfloat16), "dp", scatter_dimension=0, tiled=True
        ).astype(jnp.float32),
        lax.psum_scatter(
            grad_fc1.astype(jnp.bfloat16), "dp", scatter_dimension=0, tiled=True
        ).astype(jnp.float32),
        lax.psum_scatter(
            grad_fc2.astype(jnp.bfloat16), "dp", scatter_dimension=0, tiled=True
        ).astype(jnp.float32),
    )
    owned_grads = (
        lax.psum_scatter(
            rows_summed[0].astype(jnp.bfloat16), "mp", scatter_dimension=1, tiled=True
        ).astype(jnp.float32),
        lax.psum_scatter(
            rows_summed[1].astype(jnp.bfloat16), "mp", scatter_dimension=1, tiled=True
        ).astype(jnp.float32),
        lax.psum_scatter(
            rows_summed[2].astype(jnp.bfloat16), "mp", scatter_dimension=1, tiled=True
        ).astype(jnp.float32),
        lax.psum_scatter(
            rows_summed[3].astype(jnp.bfloat16), "mp", scatter_dimension=1, tiled=True
        ).astype(jnp.float32),
    )
    squares = jnp.zeros((), jnp.float32)
    for owned_piece in owned_grads:
        squares = squares + jnp.sum(owned_piece * owned_piece)
    kernel_squares = jnp.where(lax.axis_index("dp") == 0, jnp.sum(base_grad * base_grad), 0.0)
    table_total, square_total = lax.psum((table_grad, squares + kernel_squares), ("dp", "mp"))
    grad_norm = jnp.sqrt(square_total + jnp.sum(table_total * table_total))
    clip_level = 0.5 * math.sqrt(3 * BASE * BASE * D + 4 * D * D + 2 * D * FF + TROWS * D)
    factor = clip_level / jnp.maximum(grad_norm, clip_level)
    step_count = step[0].astype(jnp.float32)
    fix_one = 1.0 - jnp.power(BETA_ONE, step_count)
    fix_two = 1.0 - jnp.power(BETA_TWO, step_count)
    kernel_new, kernel_moments = adam_step(
        kernel_state, base_grad, rates[0], factor, fix_one, fix_two
    )
    qkv_new, qkv_moments = adam_step(qkv_state, owned_grads[0], rates[1], factor, fix_one, fix_two)
    proj_new, proj_moments = adam_step(
        proj_state, owned_grads[1], rates[2], factor, fix_one, fix_two
    )
    fc1_new, fc1_moments = adam_step(fc1_state, owned_grads[2], rates[3], factor, fix_one, fix_two)
    fc2_new, fc2_moments = adam_step(fc2_state, owned_grads[3], rates[4], factor, fix_one, fix_two)
    table_new, table_moments = adam_step(
        table_state, table_total, rates[5], factor, fix_one, fix_two
    )
    return (
        block_out,
        grad_norm,
        kernel_new,
        kernel_moments,
        qkv_new,
        qkv_moments,
        proj_new,
        proj_moments,
        fc1_new,
        fc1_moments,
        fc2_new,
        fc2_moments,
        table_new,
        table_moments,
    )


def solution(mesh):
    placed = (
        P(None, "mp", None),
        P(None, "dp", "mp"),
        P(None, "dp", "mp"),
        P(None, "dp", "mp"),
        P(None, "dp", "mp"),
        P(),
        P("dp", None, None),
        P("dp", None, None),
        P(None, "mp"),
        P(None, "mp"),
        P(),
        P(),
        P(("dp", "mp"), None),
        P(),
        P(),
    )
    return jax.shard_map(
        body,
        mesh=mesh,
        in_specs=placed,
        out_specs=(
            P(("dp", "mp"), None),
            P(),
            P("mp", None),
            P(None, "mp", None),
            P("dp", "mp"),
            P(None, "dp", "mp"),
            P("dp", "mp"),
            P(None, "dp", "mp"),
            P("dp", "mp"),
            P(None, "dp", "mp"),
            P("dp", "mp"),
            P(None, "dp", "mp"),
            P(),
            P(),
        ),
        check_vma=False,
    )
```

profile of v0, /device:TPU:0, one launch (start us, length us, event | category | flops | bytes accessed | tf_op | source)
XLA Modules:
  0.0 1532.8 jit_solution(16620727584267823737)
XLA Ops:
  17.9 39.4 %fusion.56 = f32[2304,2304]{1,0:T(8,128)} fusion(f32[2304,512]{1,0:T(8,128)} %param.28, f32[3,512,2304]{2,1,0:T(8,128)} %param.19), kind=kOutput, calls=%fused_computation.76 | convolution fusion | flops 32614907904 | bytes 30670848 | tf_op jit(solution)/shard_map/dot_general | solution.py:132
  57.2 23.5 %reshape.328 = f32[6912,768]{1,0:T(8,128)} reshape(f32[2304,2304]{1,0:T(8,128)} %fusion.56) | data formatting | bytes 42467328 | tf_op jit(solution)/shard_map/reshape | solution.py:132
  84.0 26.9 %all_gather.32 = bf16[768,384]{1,0:T(8,128)(2,1)} all-gather(bf16[48,384]{1,0:T(8,128)(2,1)S(1)} %bitcast_convert_fusion.3), channel_id=1, replica_groups=mesh['dp'=16,'mp'=2] {'dp'}, dimensions={0}, use_global_device_ids=true | all-gather | bytes 626688 | tf_op jit(solution)/shard_map/all_gather | solution.py:115
  115.4 306.2 %reduce-scatter.19.cloned.1.call-done = f32[6912,384]{1,0:T(8,128)} async-done(((f32[6912,768]{1,0:T(8,128)}), f32[6912,384]{1,0:T(8,128)}) %reduce-scatter.19.cloned.1.call-update) | async-done | bytes 10616848 | tf_op jit(solution)/shard_map/reduce_scatter | solution.py:135
  451.6 11.5 all-to-all-done
  498.3 105.5 %while.24 = (s32[]{:T(128)}, bf16[12,816,64]{1,2,0:T(8,128)(2,1)}, f32[12,816]{1,0:T(8,128)}, bf16[12,816,64]{2,1,0:T(8,128)(2,1)S(1)}, bf16[12,816,64]{2,1,0:T(...) while((s32[]{:T(128)}, bf16[12,816,64]{1,2,0:T(8,128)(2,1)}, ...), condition=%wide.region_7.8_spmd.clone, body=%wide.region_4.7_spmd.clone.sunk | while | flops 180446160 | bytes 19823804 | solution.py:181
  609.5 10.9 multiply_convert_fusion.1
  620.5 11.6 convert_reduce_fusion
  648.7 119.9 %while.25 = (s32[]{:T(128)}, bf16[12,3,816,64]{2,3,1,0:T(8,128)(2,1)}, bf16[12,816,64]{2,1,0:T(8,128)(2,1)}, bf16[12,816,64]{2,1,0:T(8,128)(2,1)}, f32[12,816]{1...) while((s32[]{:T(128)}, ...), condition=%wide.region_14.15_spmd.clone, body=%wide.region_12.14_spmd.clone.sunk | while | flops 433954496 | bytes 22510944 | solution.py:222
  819.3 11.6 reduce.22
  835.4 19.9 %all_to_all.33 = bf16[2,2,156672]{2,1,0:T(2,128)(2,1)} all-to-all(bf16[2,2,156672]{2,1,0:T(2,128)(2,1)} %reshape.357), channel_id=1, replica_groups=mesh['dp'=16,'mp'=2] {'mp'}, dimensions={0} | all-to-all | bytes 2506752 | tf_op jit(solution)/shard_map/all_to_all | solution.py:250
  876.6 48.7 %reduce-scatter.29.cloned.1.call-done = bf16[192,768]{1,0:T(8,128)(2,1)} async-done(((bf16[3072,768]{1,0:T(8,128)(2,1)}), bf16[192,768]{1,0:T(8,128)(2,1)}) %reduce-scatter.29.cloned.1.call-update) | async-done | bytes 294928 | tf_op jit(solution)/shard_map/reduce_scatter | solution.py:282
  927.3 77.6 %reduce-scatter.25.cloned.1.call-done = bf16[48,3072]{1,0:T(8,128)(2,1)} async-done(((bf16[768,3072]{1,0:T(8,128)(2,1)}), bf16[48,3072]{1,0:T(8,128)(2,1)}) %reduce-scatter.25.cloned.1.call-update) | async-done | bytes 294928 | tf_op jit(solution)/shard_map/reduce_scatter | solution.py:279
  1005.0 131.2 %all-reduce.6.cloned.1.call-done = (bf16[6912,384]{0,1:T(8,128)(2,1)}, bf16[192,384]{1,0:T(8,128)(2,1)}) async-done(((bf16[6912,384]{0,1:T(8,128)(2,1)}, bf16[192,384]{1,0:T(8,128)(2,1)}), (bf16[6912,384]{0,1:T(8,128)(2,1)}, bf16[192,384]{1,0:T(8,128)(2,1)})) %all-reduce.6.cloned.1.call-update) | async-done | bytes 5455888 | tf_op jit(solution)/shard_map/psum | solution.py:259
  1136.9 13.0 fusion.145
  1192.5 10.4 all_gather.38
  1203.0 74.2 %reduce-scatter.31.cloned.1.call-done = bf16[1152,48]{1,0:T(8,128)(2,1)} async-done(((bf16[2304,48]{1,0:T(8,128)(2,1)}), bf16[1152,48]{1,0:T(8,128)(2,1)}) %reduce-scatter.31.cloned.1.call-update) | async-done | bytes 110608
  1280.3 12.7 reduce-scatter.35.cloned.1.call-done
  1294.8 12.5 reduce-scatter.27.cloned.1.call-done
  1310.2 14.5 copy.103
  1324.7 16.5 %reshape.335 = bf16[2304,2304]{1,0:T(8,128)(2,1)} reshape(bf16[6912,768]{1,0:T(8,128)(2,1)} %copy.103) | data formatting | bytes 21233664 | tf_op jit(solution)/shard_map/reshape | solution.py:270
  1341.3 20.9 %fusion.149 = f32[2304,512]{1,0:T(8,128)S(1)} fusion(bf16[2304,2304]{1,0:T(8,128)(2,1)} %reshape.335, f32[2304,512]{1,0:T(8,128)} %param.28), kind=kOutput, calls=%fused_computation.249 | convolution fusion | flops 32614907904 | bytes 20054016 | tf_op jit(solution)/shard_map/dot_general | solution.py:46
  1368.1 69.1 %all-reduce.4.cloned.1.call-done = f32[60,768]{1,0:T(8,128)} async-done(((f32[60,768]{1,0:T(8,128)}), f32[60,768]{1,0:T(8,128)}) %all-reduce.4.cloned.1.call-update) | async-done | bytes 184336 | tf_op jit(solution)/shard_map/psum | solution.py:304
  1438.8 41.3 %psum.30 = f32[]{:T(128)} all-reduce(f32[]{:T(128)S(6)} %add.360), channel_id=1, replica_groups=mesh['dp'=16,'mp'=2] {'dp','mp'}, use_global_device_ids=true, to_apply=%region_32.33 | all-reduce | flops 1 | bytes 8 | tf_op jit(solution)/shard_map/psum | solution.py:304
  (435 shorter events, 504.2 us)
Async XLA Ops:
  8.0 413.6 %copy-start = (bf16[4,16,6912]{2,1,0:T(8,128)(2,1)S(1)}, bf16[4,16,6912]{2,1,0:T(8,128)(2,1)}, u32[]{:S(2)}) copy-start(bf16[4,16,6912]{2,1,0:T(8,128)(2,1)} %param.26) | copy-start | bytes 2654212
  8.0 74.6 %all-gather.9.cloned.1.call-start = ((), (), s32[]{:S(2)}) async-start(), calls=%async_computation.14 | async-start | bytes 1880064 | tf_op jit(solution)/shard_map/all_gather | solution.py:114
  9.8 101.2 %all-gather.15.cloned.1.call-start = ((), (), s32[]{:S(2)}) async-start(), calls=%async_computation.17 | async-start | bytes 2506752 | tf_op jit(solution)/shard_map/all_gather | solution.py:116
  11.5 102.1 %reduce-scatter.17.cloned.1.call-start = ((), (), s32[]{:S(2)}) async-start(), calls=%async_computation.12 | async-start | bytes 884736 | tf_op jit(solution)/shard_map/reduce_scatter | solution.py:134
  17.8 403.8 %reduce-scatter.19.cloned.1.call-start = ((), (), s32[]{:S(2)}) async-start(), calls=%async_computation.13 | async-start | bytes 31850496 | tf_op jit(solution)/shard_map/reduce_scatter | solution.py:135
  80.8 370.7 %all-gather.19.cloned.1.call-start = ((), (), s32[]{:S(2)}) async-start(), calls=%async_computation.19 | async-start | bytes 2506752 | tf_op jit(solution)/shard_map/all_gather | solution.py:117
  82.5 386.7 %all-gather.11.cloned.1.call-start = ((), (), s32[]{:S(2)}) async-start(), calls=%async_computation.15 | async-start | bytes 5308416 | tf_op jit(solution)/shard_map/all_gather | solution.py:120
  83.1 520.7 %all-gather.13.cloned.1.call-start = ((), (), s32[]{:S(2)}) async-start(), calls=%async_computation.16 | async-start | bytes 1769472 | tf_op jit(solution)/shard_map/all_gather | solution.py:121
  110.9 498.6 %all-gather.17.cloned.1.call-start = ((), (), s32[]{:S(2)}) async-start(), calls=%async_computation.18 | async-start | bytes 7077888 | tf_op jit(solution)/shard_map/all_gather | solution.py:122
  429.9 33.2 %all-to-all-start = ((f32[2,816,384]{2,1,0:T(8,128)}), f32[2,816,384]{2,1,0:T(8,128)S(1)}, u32[]{:S(2)}, u32[]{:S(2)}) async-start(f32[2,816,384]{2,1,0:T(8,128)} %pad_maximum_fusion.1), calls=%async_computation.2 | async-start | bytes 5013504 | tf_op jit(solution)/shard_map/all_to_all | solution.py:141
  433.7 186.8 %all-gather.21.cloned.1.call-start = ((), (), s32[]{:S(2)}) async-start(), calls=%async_computation.20 | async-start | bytes 7077888 | tf_op jit(solution)/shard_map/all_gather | solution.py:123
  451.5 421.2 %reduce-scatter.23.cloned.1.call-start = ((), (), s32[]{:S(2)}) async-start(), calls=%async_computation.22 | async-start | bytes 1253376 | tf_op jit(solution)/shard_map/reduce_scatter | solution.py:276
  609.0 179.3 %copy-start.6 = (f32[816,768]{1,0:T(8,128)}, f32[816,768]{1,0:T(8,128)S(1)}, u32[]{:S(2)}) copy-start(f32[816,768]{1,0:T(8,128)S(1)} %get-tuple-element.323) | copy-start | bytes 7520260
  648.6 225.9 %reduce-scatter.21.cloned.1.call-start = ((), (), s32[]{:S(2)}) async-start(), calls=%async_computation.21 | async-start | bytes 3760128 | tf_op jit(solution)/shard_map/reduce_scatter | solution.py:273
  779.0 146.4 %reduce-scatter.29.cloned.1.call-start = ((), (), s32[]{:S(2)}) async-start(), calls=%async_computation.25 | async-start | bytes 5013504 | tf_op jit(solution)/shard_map/reduce_scatter | solution.py:282
  788.3 216.6 %reduce-scatter.25.cloned.1.call-start = ((), (), s32[]{:S(2)}) async-start(), calls=%async_computation.23 | async-start | bytes 5013504 | tf_op jit(solution)/shard_map/reduce_scatter | solution.py:279
  798.3 337.9 %all-reduce.6.cloned.1.call-start = ((), (), s32[]{:S(2)}) async-start(), calls=%async_computation.31 | async-start | bytes 10911744 | tf_op jit(solution)/shard_map/psum | solution.py:259
  872.7 318.2 %reduce-scatter.33.cloned.1.call-start = ((), (), s32[]{:S(2)}) async-start(), calls=%async_computation.29 | async-start | bytes 294912
  874.5 402.8 %reduce-scatter.31.cloned.1.call-start = ((), (), s32[]{:S(2)}) async-start(), calls=%async_computation.28 | async-start | bytes 884736
  876.6 416.5 %reduce-scatter.35.cloned.1.call-start = ((), (), s32[]{:S(2)}) async-start(), calls=%async_computation.30 | async-start | bytes 589824
  927.2 380.1 %reduce-scatter.27.cloned.1.call-start = ((), (), s32[]{:S(2)}) async-start(), calls=%async_computation.24 | async-start | bytes 442368 | tf_op jit(solution)/shard_map/reduce_scatter | solution.py:293
  1004.9 305.3 %all-gather.23.cloned.1.call-start = ((), (), s32[]{:S(2)}) async-start(), calls=%async_computation.26 | async-start | bytes 15925248 | tf_op jit(solution)/shard_map/all_gather | solution.py:265
  1136.2 301.0 %all-reduce.4.cloned.1.call-start = ((), (), s32[]{:S(2)}) async-start(), calls=%async_computation.27 | async-start | bytes 393216 | tf_op jit(solution)/shard_map/psum | solution.py:304
  1362.2 119.3 %copy-start.15 = (f32[3,60,768]{2,1,0:T(8,128)S(1)}, f32[3,60,768]{2,1,0:T(8,128)}, u32[]{:S(2)}) copy-start(f32[3,60,768]{2,1,0:T(8,128)} %param.24) | copy-start | bytes 1658884
  (45 other events, 457.7 us)
Sparse Core Ops, SparseCore 0:
  11.6 43.0 all-gather.8
  57.5 41.2 all-gather.14
  101.7 40.7 all-gather.18
  143.9 71.4 all-gather.10
  216.7 46.7 all-gather.12
  264.9 84.6 all-gather.16
  451.6 64.0 all-gather.20
  648.8 57.9 reduce-scatter.22
  779.1 68.0 reduce-scatter.20
  850.9 74.4 reduce-scatter.28
  930.3 74.5 reduce-scatter.24
  1009.1 127.0 all-reduce.5
  1139.1 10.7 reduce-scatter.32
  1152.7 124.4 reduce-scatter.30
  1279.9 13.1 reduce-scatter.34
  1295.2 12.0 reduce-scatter.26
  1314.2 122.9 all-reduce.3
Sparse Core Ops, SparseCore 1:
  17.9 17.9 reduce-scatter.16
  80.8 340.7 reduce-scatter.18
  1136.3 134.1 all-gather.22
where the time goes:
time: 1550 us; the launch traced here: 1530 us
  waiting for transfers between devices  745 us (48%)
  matrix products  339 us (22%)
  local copies, waits for them, and re-layouts  245 us (16%)
  blocking collectives  98.5 us (6%)
  other arithmetic  76.2 us (5%)
  between operations  23.3 us (2%)
    reduce_scatter x1, waiting for transfers between devices, body(): lax.psum_scatter(part_large, 'mp', scatter_dimension=1, tiled=True)  306 us
    psum x1, waiting for transfers between devices, body(): lax.psum(kern_large_grad.astype(jnp.bfloat16), 'dp').astype(jnp.float32)  131 us
    dot_general x29, matrix products, matmul(): return jnp.dot(left, right, preferred_element_type=jnp.float32)  92.4 us
    dot_general x40, matrix products, matmul_right(): lax.dot_general(left, right, (((1,), (1,)), ((), ())), preferred_element_...  89.6 us
    unnamed x23, waiting for transfers between devices  88.2 us
    reduce_scatter x1, waiting for transfers between devices, body(): lax.psum_scatter(grad_fc1.astype(jnp.bfloat16), 'dp', scatter_dimension=0...  77.6 us
    unnamed x94, local copies, waits for them, and re-layouts  75 us
    dot_general x30, matrix products, matmul_left(): lax.dot_general(left, right, (((0,), (0,)), ((), ())), preferred_element_...  69.4 us
  transfers between devices with their start and end apart: 21, of which 9 were waited for; matrix products, arithmetic and copies ran while one was open for 37% of the time, Pallas kernels for 0%

commit v1 on v0

--- a/solution.py
+++ b/solution.py
@@ -256,7 +256,9 @@
     )
     summed_small, summed_large = (
         lax.psum(kern_small_grad.astype(jnp.bfloat16), "dp").astype(jnp.float32),
-        lax.psum(kern_large_grad.astype(jnp.bfloat16), "dp").astype(jnp.float32),
+        jnp.sum(lax.all_gather(kern_large_grad.astype(jnp.bfloat16), "dp"), axis=0).astype(
+            jnp.float32
+        ),
     )
     whole_small, whole_large = (
         lax.all_gather(summed_small.astype(jnp.bfloat16), "mp", axis=1, tiled=True).astype(

time: 1550 us -> 1920 us (1.24)
  waiting for transfers between devices: 745 us -> 976 us
  other arithmetic: 76.2 us -> 194 us
  local copies, waits for them, and re-layouts: 245 us -> 284 us
    all_gather x0 -> x1, waiting for transfers between devices: none -> 411 us  [body(): lax.all_gather(kern_large_grad.astype(jnp.bfloat16), 'dp')]
    psum x1, waiting for transfers between devices: 131 us -> 0.01 us  [body(): lax.psum(kern_small_grad.astype(jnp.bfloat16), 'dp').astype(jnp.float32)]
    reduce_sum x0 -> x1, other arithmetic: none -> 114 us  [body(): jnp.sum(lax.all_gather(kern_large_grad.astype(jnp.bfloat16), 'dp'), axis=0)]
    unnamed x23 -> x24, waiting for transfers between devices: 88.2 us -> 1.34 us
    unnamed x94 -> x109, local copies, waits for them, and re-layouts: 75 us -> 141 us
    all_gather x1, waiting for transfers between devices: 0.03 us -> 65.6 us  [body(): lax.all_gather(summed_large.astype(jnp.bfloat16), 'mp', axis=1, tiled=True)]
  transfers between devices with their start and end apart: 21 -> 22, of which waited for: 9 -> 7; matrix products, arithmetic and copies ran while one was open for 37% -> 37% of each run, Pallas kernels for 0% -> 0%
where the time goes in v1:
time: 1920 us; the launch traced here: 1910 us
  waiting for transfers between devices  976 us (51%)
  matrix products  325 us (17%)
  local copies, waits for them, and re-layouts  284 us (15%)
  other arithmetic  194 us (10%)
  blocking collectives  98.3 us (5%)
  between operations  23.6 us (1%)
    all_gather x1, waiting for transfers between devices, body(): lax.all_gather(kern_large_grad.astype(jnp.bfloat16), 'dp')  411 us
    reduce_scatter x1, waiting for transfers between devices, body(): lax.psum_scatter(part_large, 'mp', scatter_dimension=1, tiled=True)  306 us
    unnamed x109, local copies, waits for them, and re-layouts  141 us
    reduce_sum x1, other arithmetic, body(): jnp.sum(lax.all_gather(kern_large_grad.astype(jnp.bfloat16), 'dp'), axis=0)  114 us
    dot_general x40, matrix products, matmul_right(): lax.dot_general(left, right, (((1,), (1,)), ((), ())), preferred_element_...  88.8 us
    dot_general x29, matrix products, matmul(): return jnp.dot(left, right, preferred_element_type=jnp.float32)  82.1 us
    reduce_scatter x1, waiting for transfers between devices, body(): lax.psum_scatter(grad_fc1.astype(jnp.bfloat16), 'dp', scatter_dimension=0...  77.6 us
    dot_general x30, matrix products, matmul_left(): lax.dot_general(left, right, (((0,), (0,)), ((), ())), preferred_element_...  69.1 us
  transfers between devices with their start and end apart: 22, of which 7 were waited for; matrix products, arithmetic and copies ran while one was open for 37% of the time, Pallas kernels for 0%

profile of v1, /device:TPU:0, one launch (start us, length us, event | category | flops | bytes accessed | tf_op | source)
XLA Modules:
  0.0 1907.9 jit_solution(3177896528975393955)
XLA Ops:
  17.9 39.4 %fusion.56 = f32[2304,2304]{1,0:T(8,128)} fusion(f32[2304,512]{1,0:T(8,128)} %param.28, f32[3,512,2304]{2,1,0:T(8,128)} %param.19), kind=kOutput, calls=%fused_computation.77 | convolution fusion | flops 32614907904 | bytes 30670848 | tf_op jit(solution)/shard_map/dot_general | solution.py:132
  57.2 23.5 %reshape.328 = f32[6912,768]{1,0:T(8,128)} reshape(f32[2304,2304]{1,0:T(8,128)} %fusion.56) | data formatting | bytes 42467328 | tf_op jit(solution)/shard_map/reshape | solution.py:132
  84.1 26.8 %all_gather.38 = bf16[768,384]{1,0:T(8,128)(2,1)} all-gather(bf16[48,384]{1,0:T(8,128)(2,1)S(1)} %bitcast_convert_fusion.3), channel_id=1, replica_groups=mesh['dp'=16,'mp'=2] {'dp'}, dimensions={0}, use_global_device_ids=true | all-gather | bytes 626688 | tf_op jit(solution)/shard_map/all_gather | solution.py:115
  115.3 306.3 %reduce-scatter.19.cloned.1.call-done = f32[6912,384]{1,0:T(8,128)} async-done(((f32[6912,768]{1,0:T(8,128)}), f32[6912,384]{1,0:T(8,128)}) %reduce-scatter.19.cloned.1.call-update) | async-done | bytes 10616848 | tf_op jit(solution)/shard_map/reduce_scatter | solution.py:135
  451.6 11.6 all-to-all-done
  498.7 76.0 %while.24 = (s32[]{:T(128)}, bf16[12,816,64]{1,2,0:T(8,128)(2,1)}, f32[12,816]{1,0:T(8,128)}, bf16[12,816,64]{2,1,0:T(8,128)(2,1)S(1)}, bf16[12,816,64]{2,1,0:T(...) while((s32[]{:T(128)}, bf16[12,816,64]{1,2,0:T(8,128)(2,1)}, ...), condition=%wide.region_7.8_spmd.clone, body=%wide.region_4.7_spmd.clone.sunk | while | flops 180446160 | bytes 9170089 | solution.py:181
  580.5 10.9 multiply_convert_fusion.1
  591.4 11.6 convert_reduce_fusion
  618.3 120.1 %while.25 = (s32[]{:T(128)}, bf16[12,3,816,64]{2,3,1,0:T(8,128)(2,1)}, bf16[12,816,64]{2,1,0:T(8,128)(2,1)}, bf16[12,816,64]{2,1,0:T(8,128)(2,1)}, f32[12,816]{1...) while((s32[]{:T(128)}, ...), condition=%wide.region_14.15_spmd.clone, body=%wide.region_12.14_spmd.clone.sunk | while | flops 433954496 | bytes 22508920 | solution.py:222
  792.2 11.4 reduce.23
  808.1 19.7 %all_to_all.33 = bf16[2,2,156672]{2,1,0:T(2,128)(2,1)} all-to-all(bf16[2,2,156672]{2,1,0:T(2,128)(2,1)} %reshape.358), channel_id=1, replica_groups=mesh['dp'=16,'mp'=2] {'mp'}, dimensions={0} | all-to-all | bytes 2506752 | tf_op jit(solution)/shard_map/all_to_all | solution.py:250
  850.1 45.3 %reduce-scatter.29.cloned.1.call-done = bf16[192,768]{1,0:T(8,128)(2,1)} async-done(((bf16[3072,768]{1,0:T(8,128)(2,1)}), bf16[192,768]{1,0:T(8,128)(2,1)}) %reduce-scatter.29.cloned.1.call-update) | async-done | bytes 294928 | tf_op jit(solution)/shard_map/reduce_scatter | solution.py:284
  897.4 77.6 %reduce-scatter.25.cloned.1.call-done = bf16[48,3072]{1,0:T(8,128)(2,1)} async-done(((bf16[768,3072]{1,0:T(8,128)(2,1)}), bf16[48,3072]{1,0:T(8,128)(2,1)}) %reduce-scatter.25.cloned.1.call-update) | async-done | bytes 294928 | tf_op jit(solution)/shard_map/reduce_scatter | solution.py:281
  975.1 411.0 %all-gather.27.cloned.1.call-done = bf16[110592,384]{0,1:T(8,128)(2,1)} async-done(((bf16[6912,384]{0,1:T(8,128)(2,1)}), bf16[110592,384]{0,1:T(8,128)(2,1)}) %all-gather.27.cloned.1.call-update) | async-done | bytes 84934672 | tf_op jit(solution)/shard_map/all_gather | solution.py:259
  1386.1 56.8 %copy.122 = bf16[48,8,16,6912]{3,2,1,0:T(8,128)(2,1)} copy(bf16[48,8,16,6912]{3,1,2,0:T(8,128)(2,1)} %bitcast.105) | data formatting | bytes 169869312
  1442.9 113.9 %bitcast_reduce_fusion = bf16[6912,384]{0,1:T(8,128)(2,1)} fusion(bf16[48,8,16,6912]{3,2,1,0:T(8,128)(2,1)} %copy.122), kind=kLoop, calls=%fused_computation.55 | loop fusion | flops 39813120 | bytes 90243072 | tf_op jit(solution)/shard_map/reduce_sum | solution.py:259
  1556.9 13.0 fusion.145
  1625.3 65.6 %all-gather.25.cloned.1.call-done = bf16[6912,768]{0,1:T(8,128)(2,1)} async-done(((bf16[6912,384]{0,1:T(8,128)(2,1)}), bf16[6912,768]{0,1:T(8,128)(2,1)}) %all-gather.25.cloned.1.call-update) | async-done | bytes 10616848 | tf_op jit(solution)/shard_map/all_gather | solution.py:267
  1690.9 14.7 copy.101
  1705.6 16.5 reshape.335
  1722.1 20.9 %fusion.149 = f32[2304,512]{1,0:T(8,128)S(1)} fusion(bf16[2304,2304]{1,0:T(8,128)(2,1)} %reshape.335, f32[2304,512]{1,0:T(8,128)} %param.28), kind=kOutput, calls=%fused_computation.250 | convolution fusion | flops 32614907904 | bytes 20054016 | tf_op jit(solution)/shard_map/dot_general | solution.py:46
  1748.9 57.0 %all-reduce.5.cloned.1.call-done = f32[60,768]{1,0:T(8,128)} async-done(((f32[60,768]{1,0:T(8,128)}), f32[60,768]{1,0:T(8,128)}) %all-reduce.5.cloned.1.call-update) | async-done | bytes 184336 | tf_op jit(solution)/shard_map/psum | solution.py:306
  1807.5 41.4 %psum.22 = f32[]{:T(128)} all-reduce(f32[]{:T(128)S(6)} %add.358), channel_id=1, replica_groups=mesh['dp'=16,'mp'=2] {'dp','mp'}, use_global_device_ids=true, to_apply=%region_32.33 | all-reduce | flops 1 | bytes 8 | tf_op jit(solution)/shard_map/psum | solution.py:306
  1850.2 12.3 fusion.70
  (430 shorter events, 476.0 us)
Async XLA Ops:
  8.0 413.6 %copy-start = (bf16[4,16,6912]{2,1,0:T(8,128)(2,1)S(1)}, bf16[4,16,6912]{2,1,0:T(8,128)(2,1)}, u32[]{:S(2)}) copy-start(bf16[4,16,6912]{2,1,0:T(8,128)(2,1)} %param.26) | copy-start | bytes 2654212
  8.0 74.6 %all-gather.11.cloned.1.call-start = ((), (), s32[]{:S(2)}) async-start(), calls=%async_computation.14 | async-start | bytes 1880064 | tf_op jit(solution)/shard_map/all_gather | solution.py:114
  9.8 101.2 %all-gather.17.cloned.1.call-start = ((), (), s32[]{:S(2)}) async-start(), calls=%async_computation.17 | async-start | bytes 2506752 | tf_op jit(solution)/shard_map/all_gather | solution.py:116
  11.5 102.0 %reduce-scatter.17.cloned.1.call-start = ((), (), s32[]{:S(2)}) async-start(), calls=%async_computation.12 | async-start | bytes 884736 | tf_op jit(solution)/shard_map/reduce_scatter | solution.py:134
  17.8 403.8 %reduce-scatter.19.cloned.1.call-start = ((), (), s32[]{:S(2)}) async-start(), calls=%async_computation.13 | async-start | bytes 31850496 | tf_op jit(solution)/shard_map/reduce_scatter | solution.py:135
  80.8 370.8 %all-gather.21.cloned.1.call-start = ((), (), s32[]{:S(2)}) async-start(), calls=%async_computation.19 | async-start | bytes 2506752 | tf_op jit(solution)/shard_map/all_gather | solution.py:117
  82.5 387.3 %all-gather.13.cloned.1.call-start = ((), (), s32[]{:S(2)}) async-start(), calls=%async_computation.15 | async-start | bytes 5308416 | tf_op jit(solution)/shard_map/all_gather | solution.py:120
  83.1 491.7 %all-gather.15.cloned.1.call-start = ((), (), s32[]{:S(2)}) async-start(), calls=%async_computation.16 | async-start | bytes 1769472 | tf_op jit(solution)/shard_map/all_gather | solution.py:121
  110.9 469.7 %all-gather.19.cloned.1.call-start = ((), (), s32[]{:S(2)}) async-start(), calls=%async_computation.18 | async-start | bytes 7077888 | tf_op jit(solution)/shard_map/all_gather | solution.py:122
  429.9 33.4 %all-to-all-start = ((f32[2,816,384]{2,1,0:T(8,128)}), f32[2,816,384]{2,1,0:T(8,128)S(1)}, u32[]{:S(2)}, u32[]{:S(2)}) async-start(f32[2,816,384]{2,1,0:T(8,128)} %pad_maximum_fusion.1), calls=%async_computation.2 | async-start | bytes 5013504 | tf_op jit(solution)/shard_map/all_to_all | solution.py:141
  433.8 157.6 %all-gather.23.cloned.1.call-start = ((), (), s32[]{:S(2)}) async-start(), calls=%async_computation.20 | async-start | bytes 7077888 | tf_op jit(solution)/shard_map/all_gather | solution.py:123
  451.6 394.6 %reduce-scatter.23.cloned.1.call-start = ((), (), s32[]{:S(2)}) async-start(), calls=%async_computation.22 | async-start | bytes 1253376 | tf_op jit(solution)/shard_map/reduce_scatter | solution.py:278
  618.3 229.8 %reduce-scatter.21.cloned.1.call-start = ((), (), s32[]{:S(2)}) async-start(), calls=%async_computation.21 | async-start | bytes 3760128 | tf_op jit(solution)/shard_map/reduce_scatter | solution.py:275
  618.3 120.1 %copy-start.3 = (f32[1,816,2,384]{3,1,2,0:T(8,128)S(1)}, f32[1,816,2,384]{3,1,2,0:T(8,128)}, u32[]{:S(2)}) copy-start(f32[1,816,2,384]{3,1,2,0:T(8,128)} %copy-done.2) | copy-start | bytes 7520260
  749.0 146.4 %reduce-scatter.29.cloned.1.call-start = ((), (), s32[]{:S(2)}) async-start(), calls=%async_computation.25 | async-start | bytes 5013504 | tf_op jit(solution)/shard_map/reduce_scatter | solution.py:284
  760.1 214.8 %reduce-scatter.25.cloned.1.call-start = ((), (), s32[]{:S(2)}) async-start(), calls=%async_computation.23 | async-start | bytes 5013504 | tf_op jit(solution)/shard_map/reduce_scatter | solution.py:281
  771.7 614.4 %all-gather.27.cloned.1.call-start = ((), (), s32[]{:S(2)}) async-start(), calls=%async_computation.29 | async-start | bytes 90243072 | tf_op jit(solution)/shard_map/all_gather | solution.py:259
  842.6 762.7 %all-reduce.3.cloned.1.call-start = ((), (), s32[]{:S(2)}) async-start(), calls=%async_computation.26 | async-start | bytes 294912 | tf_op jit(solution)/shard_map/psum | solution.py:258
  846.2 769.8 %reduce-scatter.33.cloned.1.call-start = ((), (), s32[]{:S(2)}) async-start(), calls=%async_computation.31 | async-start | bytes 294912
  848.0 769.6 %reduce-scatter.31.cloned.1.call-start = ((), (), s32[]{:S(2)}) async-start(), calls=%async_computation.30 | async-start | bytes 884736
  850.1 770.6 %reduce-scatter.35.cloned.1.call-start = ((), (), s32[]{:S(2)}) async-start(), calls=%async_computation.32 | async-start | bytes 589824
  897.3 725.1 %reduce-scatter.27.cloned.1.call-start = ((), (), s32[]{:S(2)}) async-start(), calls=%async_computation.24 | async-start | bytes 442368 | tf_op jit(solution)/shard_map/reduce_scatter | solution.py:295
  975.0 715.9 %all-gather.25.cloned.1.call-start = ((), (), s32[]{:S(2)}) async-start(), calls=%async_computation.27 | async-start | bytes 15925248 | tf_op jit(solution)/shard_map/all_gather | solution.py:267
  1556.9 249.0 %all-reduce.5.cloned.1.call-start = ((), (), s32[]{:S(2)}) async-start(), calls=%async_computation.28 | async-start | bytes 393216 | tf_op jit(solution)/shard_map/psum | solution.py:306
  (41 other events, 264.4 us)
Sparse Core Ops, SparseCore 0:
  11.6 43.0 all-gather.10
  57.6 41.1 all-gather.16
  101.7 40.8 all-gather.20
  143.9 71.4 all-gather.12
  216.7 46.7 all-gather.14
  264.9 84.6 all-gather.18
  451.7 64.0 all-gather.22
  618.4 58.0 reduce-scatter.22
  749.2 67.9 reduce-scatter.20
  820.9 74.5 reduce-scatter.28
  900.4 74.5 reduce-scatter.24
  977.0 409.0 all-gather.26
  1390.1 87.7 all-reduce.2
  1480.6 11.8 reduce-scatter.32
  1495.2 15.2 reduce-scatter.30
  1513.2 13.1 reduce-scatter.34
  1528.4 12.0 reduce-scatter.26
  1595.3 210.5 all-reduce.4
Sparse Core Ops, SparseCore 1:
  17.9 17.9 reduce-scatter.16
  80.8 340.7 reduce-scatter.18
  1557.0 133.9 all-gather.24
